TPU v7x, 32 devices: a whole 2x2x4 slice. The times are simulated.
32 devices in a mesh: wide: 8 (over z, x), narrow: 4 (over y, core).
Axes of the slice: x: 2, y: 2, z: 4, core: 2. Of those that a mesh axis runs over, the one named last changes fastest.
Arguments:
- tokens: bfloat16 [512, 8192], P('wide', 'narrow'), may hold values from -6 to 6
- grad_out: bfloat16 [512, 8192], P('wide', 'narrow'), may hold values from -6 to 6
- gate_weight: bfloat16 [8192, 24576], P('narrow', 'wide'), may hold values from -0.15625 to 0.15625
- up_weight: bfloat16 [8192, 24576], P('narrow', 'wide'), may hold values from -0.15625 to 0.15625
- down_weight: bfloat16 [24576, 8192], P('wide', 'narrow'), may hold values from -0.078125 to 0.078125
- block_mask: int32 [3, 64, 192], P(None, 'narrow', 'wide'), may hold values 0 or 1
Outputs:
- output: bfloat16 [512, 8192], P('wide', 'narrow')
- input_grad: bfloat16 [512, 8192], P('wide', 'narrow')
- gate_wgrad: bfloat16 [8192, 24576], P('narrow', 'wide')
- up_wgrad: bfloat16 [8192, 24576], P('narrow', 'wide')
- down_wgrad: bfloat16 [24576, 8192], P('wide', 'narrow')
All inputs are finite; a program needn't handle non-finite values. No bound on the sum of `block_mask` on one device may be relied on, other than what follows from the above.
Results may differ from a plain program's by a relative error of at most 0.0051.
Values may be sent and summed in bfloat16 or wider, within the bound.
No kernel may reach another device: no remote copies, remote signals or barrier semaphores. Data moves between devices by JAX's collectives and lax.ppermute only.
A program may use at most 256 MiB of HBM per device.

v0:
```python
import jax
import jax.numpy as jnp
from jax import lax
from jax.sharding import PartitionSpec as P


def expand_mask(blocks, height, width, dtype):
    tall = jnp.repeat(blocks, height // blocks.shape[0], axis=0)
    return jnp.repeat(tall, width // blocks.shape[1], axis=1).astype(dtype)


def contract_first(left, right):
    return lax.dot_general(
        left, right, (((0,), (0,)), ((), ())), preferred_element_type=jnp.float32
    )


def contract_last(left, right):
    return lax.dot_general(
        left, right, (((1,), (1,)), ((), ())), preferred_element_type=jnp.float32
    )


def body(tokens, grad_out, gate_weight, up_weight, down_weight, block_mask):
    wtype = gate_weight.dtype
    mask_gate = expand_mask(block_mask[0], gate_weight.shape[0], gate_weight.shape[1], wtype)
    mask_up = expand_mask(block_mask[1], up_weight.shape[0], up_weight.shape[1], wtype)
    mask_down = expand_mask(block_mask[2].T, down_weight.shape[0], down_weight.shape[1], wtype)
    gate_masked = gate_weight * mask_gate
    up_masked = up_weight * mask_up
    down_masked = down_weight * mask_down
    inputs_all, cotan_all = (
        lax.all_gather(tokens, "wide", axis=0, tiled=True),
        lax.all_gather(grad_out, "wide", axis=0, tiled=True),
    )
    gate_part = jnp.dot(inputs_all, gate_masked, preferred_element_type=jnp.float32)
    up_part = jnp.dot(inputs_all, up_masked, preferred_element_type=jnp.float32)
    gate_pre, up_pre = lax.psum((gate_part, up_part), "narrow")
    sig = jax.nn.sigmoid(gate_pre)
    hidden = (gate_pre * sig * up_pre).astype(jnp.bfloat16)
    output = lax.psum_scatter(
        jnp.dot(hidden, down_masked, preferred_element_type=jnp.float32),
        "wide",
        scatter_dimension=0,
        tiled=True,
    ).astype(jnp.bfloat16)
    grad_part = contract_last(cotan_all, down_masked)
    hidden_grad = lax.psum(grad_part, "narrow")
    gate_grad = (hidden_grad * up_pre * sig * (1.0 + gate_pre * (1.0 - sig))).astype(jnp.bfloat16)
    up_grad = (hidden_grad * gate_pre * sig).astype(jnp.bfloat16)
    input_grad = lax.psum_scatter(
        contract_last(gate_grad, gate_masked) + contract_last(up_grad, up_masked),
        "wide",
        scatter_dimension=0,
        tiled=True,
    ).astype(jnp.bfloat16)
    gate_wgrad = (contract_first(inputs_all, gate_grad) * mask_gate).astype(jnp.bfloat16)
    up_wgrad = (contract_first(inputs_all, up_grad) * mask_up).astype(jnp.bfloat16)
    down_wgrad = (contract_first(hidden, cotan_all) * mask_down).astype(jnp.bfloat16)
    return (output, input_grad, gate_wgrad, up_wgrad, down_wgrad)


def solution(mesh):
    return jax.shard_map(
        body,
        mesh=mesh,
        in_specs=(
            P("wide", "narrow"),
            P("wide", "narrow"),
            P("narrow", "wide"),
            P("narrow", "wide"),
            P("wide", "narrow"),
            P(None, "narrow", "wide"),
        ),
        out_specs=(
            P("wide", "narrow"),
            P("wide", "narrow"),
            P("narrow", "wide"),
            P("narrow", "wide"),
            P("wide", "narrow"),
        ),
        check_vma=False,
    )
```

profile of v0, /device:TPU:0, one launch (start us, length us, event | category | flops | bytes accessed | tf_op | source)
XLA Modules:
  0.0 675.5 jit_solution(11426675154637220597)
XLA Ops:
  10.0 16.6 %copy.12 = bf16[2048,3072]{0,1:T(8,128)(2,1)} copy(bf16[2048,3072]{1,0:T(8,128)(2,1)} %param.8) | data formatting | bytes 25165824 | tf_op args[2]
  26.7 16.6 %copy.14 = bf16[2048,3072]{0,1:T(8,128)(2,1)} copy(bf16[2048,3072]{1,0:T(8,128)(2,1)} %param.9) | data formatting | bytes 25165824 | tf_op args[3]
  43.3 11.1 %bitcast_multiply_fusion.3 = bf16[2048,3072]{0,1:T(8,128)(2,1)} fusion(bf16[2048,3072]{0,1:T(8,128)(2,1)} %copy.12, bf16[2048,24]{0,1:T(8,128)(2,1)S(1)} %bitcast.69), kind=kLoop, calls=%fused_computation.6 | loop fusion | flops 6291456 | bytes 25264128 | tf_op jit(solution)/shard_map/mul | solution.py:29
  54.4 1.9 copy-done
  56.3 5.1 bitcast_multiply_fusion.2
  62.1 12.2 %convolution_bitcast_fusion.2 = f32[512,3072]{0,1:T(8,128)} fusion(bf16[2048,3072]{0,1:T(8,128)(2,1)} %bitcast_multiply_fusion.3, bf16[512,2048]{1,0:T(8,128)(2,1)} %all-gather.3.cloned.1.call-done), kind=kOutput, calls=%fused_computation.14 | convolution fusion | flops 6442450944 | bytes 20971520 | tf_op jit(solution)/shard_map/dot_general | solution.py:36
  74.3 9.0 %convolution_bitcast_fusion.1 = f32[512,3072]{0,1:T(8,128)} fusion(bf16[2048,3072]{0,1:T(8,128)(2,1)S(1)} %copy-done.2, bf16[512,2048]{1,0:T(8,128)(2,1)S(1)} %copy-done.5), kind=kOutput, calls=%fused_computation.13 | convolution fusion | flops 6442450944 | bytes 20971520 | tf_op jit(solution)/shard_map/dot_general | solution.py:37
  83.3 28.7 %all-gather.5.cloned.1.call-done = bf16[512,2048]{1,0:T(8,128)(2,1)} async-done(((bf16[64,2048]{1,0:T(8,128)(2,1)}), bf16[512,2048]{1,0:T(8,128)(2,1)}) %all-gather.5.cloned.1.call-update) | async-done | bytes 2097168 | tf_op jit(solution)/shard_map/all_gather | solution.py:34
  112.2 7.8 %broadcast_in_dim.23 = bf16[3072,16,128]{2,1,0:T(8,128)(2,1)S(1)} broadcast(bf16[3072,16]{1,0:T(8,128)(2,1)S(1)} %bitcast.68), dimensions={0,1} | broadcast | bytes 12681216 | tf_op jit(solution)/shard_map/broadcast_in_dim | solution.py:9
  120.0 4.5 copy-done.1
  124.5 12.3 %convolution_bitcast_fusion = f32[512,3072]{0,1:T(8,128)} fusion(bf16[512,2048]{1,0:T(8,128)(2,1)} %all-gather.5.cloned.1.call-done, bf16[3072,2048]{1,0:T(8,128)(2,1)} %param.10, bf16[384,8,16,128]{3,2,1,0:T(8,128)(2,1)S(1)} %bitcast.63), kind=kOutput, calls=%fused_computation.12 | convolution fusion | flops 6448742400 | bytes 33554432 | tf_op jit(solution)/shard_map/dot_general | solution.py:19
  136.9 321.5 %all-reduce.3.cloned.1.call-done = (f32[512,3072]{0,1:T(8,128)}, f32[512,3072]{0,1:T(8,128)}, f32[512,3072]{0,1:T(8,128)}) async-done(((f32[512,3072]{0,1:T(8,128)}, f32[512,3072]{0,1:T(8,128)}, f32[512,3072]{0,1:T(8,128)}), (f32[512,3072]{0,1:T(8,128)}, f32[512,3072]{0,1:T(8,128)}, f32[512,3072]{0,1:T(8,128)})) %all-reduce.3.cloned.1.call-update) | async-done | bytes 18874384 | tf_op jit(solution)/shard_map/psum | solution.py:38
  458.3 8.6 %multiply_convert_fusion.1 = (bf16[512,3072]{0,1:T(8,128)(2,1)S(1)}, bf16[512,3072]{0,1:T(8,128)(2,1)S(1)}, bf16[512,3072]{0,1:T(8,128)(2,1)S(1)}) fusion(f32[512,3072]{0,1:T(8,128)} %get-tuple-element.12, f32[512,3072]{0,1:T(8,128)} %get-tuple-element.11, f32[512,3072]{0,1:T(8,128)} %get-tuple-element.10), kind=kLoop, calls=%fused_computation.8 | loop fusion | flops 25165824 | bytes 28311552 | tf_op jit(solution)/shard_map/convert_element_type | solution.py:50
  467.0 12.2 %fusion.3 = f32[512,2048]{1,0:T(8,128)S(1)} fusion(bf16[512,3072]{0,1:T(8,128)(2,1)S(1)} %get-tuple-element.14, bf16[2048,3072]{0,1:T(8,128)(2,1)} %bitcast_multiply_fusion.3), kind=kOutput, calls=%fused_computation.22 | convolution fusion | flops 6442450944 | bytes 19922944 | tf_op jit(solution)/shard_map/dot_general | solution.py:19
  479.3 8.3 %convolution_add_fusion = f32[512,2048]{1,0:T(8,128)} fusion(f32[512,2048]{1,0:T(8,128)S(1)} %fusion.3, bf16[512,3072]{0,1:T(8,128)(2,1)S(1)} %get-tuple-element.13, bf16[2048,3072]{0,1:T(8,128)(2,1)S(1)} %bitcast.67), kind=kOutput, calls=%fused_computation.16 | convolution fusion | flops 6443499520 | bytes 24117248 | tf_op jit(solution)/shard_map/dot_general | solution.py:19
  487.7 15.0 %fusion.2 = f32[512,2048]{1,0:T(8,128)} fusion(bf16[512,3072]{0,1:T(8,128)(2,1)S(1)} %get-tuple-element.15, bf16[3072,2048]{1,0:T(8,128)(2,1)} %param.10, bf16[384,8,16,128]{3,2,1,0:T(8,128)(2,1)} %bitcast.64), kind=kOutput, calls=%fused_computation.15 | convolution fusion | flops 6448742400 | bytes 32505856 | tf_op jit(solution)/shard_map/dot_general | solution.py:42
  502.7 11.9 %fusion = bf16[2048,3072]{0,1:T(8,128)(2,1)} fusion(bf16[512,3072]{0,1:T(8,128)(2,1)} %copy-done.4, bf16[512,2048]{1,0:T(8,128)(2,1)} %all-gather.3.cloned.1.call-done, bf16[2048,24]{0,1:T(8,128)(2,1)S(1)} %bitcast.72), kind=kOutput, calls=%fused_computation.1 | convolution fusion | flops 6461325312 | bytes 17924096 | tf_op jit(solution)/shard_map/dot_general | solution.py:13
  514.6 16.6 %copy.17 = bf16[2048,3072]{1,0:T(8,128)(2,1)} copy(bf16[2048,3072]{0,1:T(8,128)(2,1)} %fusion) | data formatting | bytes 25165824
  531.2 11.9 %fusion.1 = bf16[2048,3072]{0,1:T(8,128)(2,1)} fusion(bf16[512,3072]{0,1:T(8,128)(2,1)} %copy-done.3, bf16[512,2048]{1,0:T(8,128)(2,1)} %all-gather.3.cloned.1.call-done, bf16[2048,24]{0,1:T(8,128)(2,1)S(1)} %bitcast.70), kind=kOutput, calls=%fused_computation.3 | convolution fusion | flops 6461325312 | bytes 17924096 | tf_op jit(solution)/shard_map/dot_general | solution.py:13
  543.1 16.7 %copy.16 = bf16[2048,3072]{1,0:T(8,128)(2,1)} copy(bf16[2048,3072]{0,1:T(8,128)(2,1)} %fusion.1) | data formatting | bytes 25165824
  559.8 13.8 %multiply_convert_fusion = bf16[3072,2048]{1,0:T(8,128)(2,1)} fusion(bf16[512,3072]{0,1:T(8,128)(2,1)S(1)} %get-tuple-element.15, bf16[512,2048]{1,0:T(8,128)(2,1)} %all-gather.5.cloned.1.call-done, bf16[384,8,16,128]{3,2,1,0:T(8,128)(2,1)} %bitcast.65), kind=kOutput, calls=%fused_computation.4 | convolution fusion | flops 6461325312 | bytes 30408704 | tf_op jit(solution)/shard_map/dot_general | solution.py:13
  573.5 2.3 reduce-scatter.5.cloned.1.call-done
  575.9 1.8 convert_element_type.86
  577.6 89.5 %reduce-scatter.3.cloned.1.call-done = f32[64,2048]{1,0:T(8,128)} async-done(((f32[512,2048]{1,0:T(8,128)}), f32[64,2048]{1,0:T(8,128)}) %reduce-scatter.3.cloned.1.call-update) | async-done | bytes 524304 | tf_op jit(solution)/shard_map/reduce_scatter | solution.py:41
  (39 shorter events, 5.6 us)
Async XLA Ops:
  7.2 55.0 %all-gather.3.cloned.1.call-start = ((), (), s32[]{:S(2)}) async-start(), calls=%async_computation.2 | async-start | bytes 2359296 | tf_op jit(solution)/shard_map/all_gather | solution.py:33
  7.9 104.2 %all-gather.5.cloned.1.call-start = ((), (), s32[]{:S(2)}) async-start(), calls=%async_computation.4 | async-start | bytes 2359296 | tf_op jit(solution)/shard_map/all_gather | solution.py:34
  8.7 449.7 %all-reduce.3.cloned.1.call-start = ((), (), s32[]{:S(2)}) async-start(), calls=%async_computation.6 | async-start | bytes 37748736 | tf_op jit(solution)/shard_map/psum | solution.py:38
  43.3 13.0 %copy-start = (bf16[2048,3072]{0,1:T(8,128)(2,1)S(1)}, bf16[2048,3072]{0,1:T(8,128)(2,1)}, u32[]{:S(2)}) copy-start(bf16[2048,3072]{0,1:T(8,128)(2,1)} %copy.14) | copy-start | bytes 37748740
  62.1 12.2 %copy-start.2 = (bf16[2048,3072]{0,1:T(8,128)(2,1)S(1)}, bf16[2048,3072]{0,1:T(8,128)(2,1)}, u32[]{:S(2)}) copy-start(bf16[2048,3072]{0,1:T(8,128)(2,1)} %bitcast_multiply_fusion.2) | copy-start | bytes 37748740
  62.1 12.2 %copy-start.5 = (bf16[512,2048]{1,0:T(8,128)(2,1)S(1)}, bf16[512,2048]{1,0:T(8,128)(2,1)}, u32[]{:S(2)}) copy-start(bf16[512,2048]{1,0:T(8,128)(2,1)} %all-gather.3.cloned.1.call-done) | copy-start | bytes 6291460
  119.9 4.5 copy-start.1
  136.8 439.0 %reduce-scatter.5.cloned.1.call-start = ((), (), s32[]{:S(2)}) async-start(), calls=%async_computation.5 | async-start | bytes 4718592 | tf_op jit(solution)/shard_map/reduce_scatter | solution.py:51
  458.3 20.9 %slice-start = ((s8[12582912]{0:T(1024)(128)(4,1)}), s8[4194304]{0:T(1024)(128)(4,1)S(1)}, s32[]{:S(2)}) async-start(s8[12582912]{0:T(1024)(128)(4,1)} %bitcast.66), calls=%async_computation.7 | async-start | bytes 8388608
  458.3 20.9 %slice-start.1 = ((s8[12582912]{0:T(1024)(128)(4,1)}), s8[4194304]{0:T(1024)(128)(4,1)S(1)}, s32[]{:S(2)}) async-start(s8[12582912]{0:T(1024)(128)(4,1)} %bitcast.66), calls=%async_computation.8 | async-start | bytes 8388608
  466.9 12.3 %copy-start.3 = (bf16[512,3072]{0,1:T(8,128)(2,1)}, bf16[512,3072]{0,1:T(8,128)(2,1)S(1)}, u32[]{:S(2)}) copy-start(bf16[512,3072]{0,1:T(8,128)(2,1)S(1)} %get-tuple-element.14) | copy-start | bytes 9437188
  466.9 12.3 %copy-start.4 = (bf16[512,3072]{0,1:T(8,128)(2,1)}, bf16[512,3072]{0,1:T(8,128)(2,1)S(1)}, u32[]{:S(2)}) copy-start(bf16[512,3072]{0,1:T(8,128)(2,1)S(1)} %get-tuple-element.13) | copy-start | bytes 9437188
  466.9 12.3 %slice-start.2 = ((s8[12582912]{0:T(1024)(128)(4,1)}), s8[4194304]{0:T(1024)(128)(4,1)S(1)}, s32[]{:S(2)}) async-start(s8[12582912]{0:T(1024)(128)(4,1)} %bitcast.66), calls=%async_computation.9 | async-start | bytes 8388608
  487.6 179.6 %reduce-scatter.3.cloned.1.call-start = ((), (), s32[]{:S(2)}) async-start(), calls=%async_computation.3 | async-start | bytes 4718592 | tf_op jit(solution)/shard_map/reduce_scatter | solution.py:41
Sparse Core Ops, SparseCore 0:
  10.1 51.9 all-gather.2
  64.3 47.7 all-gather.4
  136.9 321.3 all-reduce.2
  487.7 88.0 reduce-scatter.4
  579.3 87.7 reduce-scatter.2
where the time goes:
time: 677 us; the launch traced here: 675 us
  waiting for transfers between devices  444 us (66%)
  matrix products  107 us (16%)
  local copies, waits for them, and re-layouts  81.4 us (12%)
  other arithmetic  29 us (4%)
  between operations  13.9 us (2%)
    psum x1, waiting for transfers between devices, body(): gate_pre, up_pre = lax.psum((gate_part, up_part), 'narrow')  321 us
    reduce_scatter x1, waiting for transfers between devices, body(): lax.psum_scatter(jnp.dot(hidden, down_masked, preferred_element_type=jnp....  89.5 us
    unnamed x24, local copies, waits for them, and re-layouts  73.1 us
    dot_general x3, matrix products, contract_first(): lax.dot_general(left, right, (((0,), (0,)), ((), ())), preferred_element_...  37.5 us
    dot_general x3, matrix products, contract_last(): lax.dot_general(left, right, (((1,), (1,)), ((), ())), preferred_element_...  32.9 us
    all_gather x1, waiting for transfers between devices, body(): lax.all_gather(grad_out, 'wide', axis=0, tiled=True)  28.7 us
    dot_general x1, matrix products, body(): jnp.dot(hidden, down_masked, preferred_element_type=jnp.float32)  15 us
  transfers between devices with their start and end apart: 5, of which 5 were waited for; matrix products, arithmetic and copies ran while one was open for 24% of the time, Pallas kernels for 0%

commit v1 on v0

--- a/solution.py
+++ b/solution.py
@@ -1,7 +1,20 @@
+import functools
+
 import jax
 import jax.numpy as jnp
 from jax import lax
+from jax.experimental import pallas as pl
+from jax.experimental.pallas import tpu as pltpu
 from jax.sharding import PartitionSpec as P
+
+F32, BF16 = jnp.float32, jnp.bfloat16
+SIDE = 128
+TILE = 512
+CHUNKS = 4
+GROUP = 8
+PIECE = 8
+UNROLL = 4
+VMEM = 56 * 1024 * 1024
 
 
 def expand_mask(blocks, height, width, dtype):
@@ -21,7 +34,7 @@
     )
 
 
-def body(tokens, grad_out, gate_weight, up_weight, down_weight, block_mask):
+def plain_body(tokens, grad_out, gate_weight, up_weight, down_weight, block_mask):
     wtype = gate_weight.dtype
     mask_gate = expand_mask(block_mask[0], gate_weight.shape[0], gate_weight.shape[1], wtype)
     mask_up = expand_mask(block_mask[1], up_weight.shape[0], up_weight.shape[1], wtype)
@@ -60,7 +73,384 @@
     return (output, input_grad, gate_wgrad, up_wgrad, down_wgrad)
 
 
+def tables(mask):
+    count = mask.shape[1]
+    kept = mask != 0
+    before = jnp.arange(count)[:, None] < jnp.arange(count)[None, :]
+    rank = jnp.sum(kept[:, :, None, :] & before[None, :, :, None], axis=1)
+    slots = -(-count // GROUP) * GROUP
+    hit = kept[:, :, None, :] & (rank[:, :, None, :] == jnp.arange(slots)[None, None, :, None])
+    gap = count - jnp.arange(count)
+    slot = count - jnp.sum(jnp.where(hit, gap[None, :, None, None], 0), axis=1)
+    each = jnp.sum(kept, axis=1)
+    wide = jnp.arange(mask.shape[2])
+    ends = jnp.sum(jnp.where(wide[None, :, None] < jnp.arange(mask.shape[2] + 1)[None, None, :], each[:, :, None], 0), axis=1)
+    slot = jnp.transpose(slot, (0, 2, 1)).astype(jnp.int32)
+    return slot.reshape(slot.shape[0] * slot.shape[1], slots), ends.astype(jnp.int32)
+
+
+def pack_kernel(slot1, ends1, slot2, ends2, gate_ref, up_ref, down_ref, *refs):
+    lists, sem = refs[:6], refs[6]
+
+    def copies(act):
+        for which in range(6):
+            first = which < 3
+            matrix = which % 3
+            slot, ends = (slot1, ends1) if first else (slot2, ends2)
+            weight = (gate_ref, up_ref, down_ref)[matrix]
+            columns = ends.shape[1] - 1
+            straight = first == (matrix < 2)
+
+            def column(j, carry):
+                start = ends[matrix, j]
+
+                def block(s, inner):
+                    k = slot[matrix * columns + j, s]
+                    row, col = (k, j) if straight else (j, k)
+                    act(pltpu.make_async_copy(
+                        weight.at[pl.ds(pl.multiple_of(row * SIDE, SIDE), SIDE), pl.ds(pl.multiple_of(col * SIDE, SIDE), SIDE)],
+                        lists[which].at[start + s],
+                        sem,
+                    ))
+                    return inner
+
+                return lax.fori_loop(0, ends[matrix, j + 1] - start, block, carry)
+
+            lax.fori_loop(0, columns, column, 0)
+
+    copies(lambda copy: copy.start())
+    copies(lambda copy: copy.wait())
+
+
+def pack_blocks(weights, first, second):
+    blocks = weights[0].shape[0] // SIDE * (weights[0].shape[1] // SIDE)
+    shape = jax.ShapeDtypeStruct((-(-blocks // PIECE) * PIECE + PIECE, SIDE, SIDE), BF16)
+    return pl.pallas_call(
+        pack_kernel,
+        grid_spec=pltpu.PrefetchScalarGridSpec(
+            num_scalar_prefetch=4,
+            grid=(1,),
+            in_specs=[pl.BlockSpec(memory_space=pl.ANY)] * 3,
+            out_specs=[pl.BlockSpec(memory_space=pl.ANY)] * 6,
+            scratch_shapes=[pltpu.SemaphoreType.DMA(())],
+        ),
+        out_shape=[shape] * 6,
+        cost_estimate=pl.CostEstimate(flops=0, bytes_accessed=60_000_000, transcendentals=0),
+        name="pack_blocks",
+    )(*first, *second, *weights)
+
+
+def fetch_pieces(ends, lists, bufs, sems, act):
+    for i in range(3):
+        total = ends[i, ends.shape[1] - 1]
+
+        def piece(p, carry):
+            where = pl.ds(p * PIECE, PIECE)
+            act(i, pltpu.make_async_copy(lists[i].at[where], bufs[i].at[where], sems.at[i]))
+            return carry
+
+        lax.fori_loop(0, (total + PIECE - 1) // PIECE, piece, 0)
+
+
+def wait_pieces(ends, lists, bufs, sems, i):
+    total = ends[i, ends.shape[1] - 1]
+
+    def piece(p, carry):
+        where = pl.ds(p * PIECE, PIECE)
+        pltpu.make_async_copy(lists[i].at[where], bufs[i].at[where], sems.at[i]).wait()
+        return carry
+
+    lax.fori_loop(0, (total + PIECE - 1) // PIECE, piece, 0)
+    bufs[i][pl.ds(total, GROUP)] = jnp.zeros((GROUP, SIDE, SIDE), BF16)
+
+
+def group_dot(slot, ends, i, j, g, left, buf, straight):
+    columns = ends.shape[1] - 1
+    start = ends[i, j] + g * GROUP
+    acts = jnp.concatenate([left[slot[i * columns + j, g * GROUP + s]] for s in range(GROUP)], axis=1)
+    if straight:
+        block = buf[pl.ds(start, GROUP)].reshape(GROUP * SIDE, SIDE)
+        return jnp.dot(acts, block, preferred_element_type=F32)
+    block = jnp.concatenate([buf[start + s] for s in range(GROUP)], axis=1)
+    return contract_last(acts, block)
+
+
+def more_groups(slot, ends, i, j, left, buf, straight, add):
+    groups = (ends[i, j + 1] - ends[i, j] + GROUP - 1) // GROUP
+
+    @pl.when(groups > 1)
+    def _():
+        def body(g, carry):
+            add(group_dot(slot, ends, i, j, g, left, buf, straight))
+            return carry
+
+        lax.fori_loop(1, groups, body, 0)
+
+
+def pre_kernel(core_ref, slot, ends, x_ref, g_ref, *refs):
+    lists, (send_ref, keep_ref), bufs, (xs, gs, sems) = refs[:3], refs[3:5], refs[5:8], refs[8:]
+    fetch_pieces(ends, lists, bufs, sems, lambda i, copy: copy.start())
+    blocks = x_ref.shape[1] // SIDE
+    for ref, scratch in ((x_ref, xs), (g_ref, gs)):
+        for k in range(blocks):
+            scratch[k] = ref[:, k * SIDE:(k + 1) * SIDE]
+        scratch[blocks] = jnp.zeros(scratch.shape[1:], BF16)
+    half = send_ref.shape[2] // SIDE
+    core = core_ref[0]
+    for i in range(3):
+        wait_pieces(ends, lists, bufs, sems, i)
+        left, straight = (xs, True) if i < 2 else (gs, False)
+        for out, base in ((send_ref, half * (1 - core)), (keep_ref, half * core)):
+            def some(t, carry):
+                for u in range(UNROLL):
+                    q = t * UNROLL + u
+                    value = group_dot(slot, ends, i, base + q, 0, left, bufs[i], straight)
+                    out[i, :, pl.ds(pl.multiple_of(q * SIDE, SIDE), SIDE)] = value
+                return carry
+
+            lax.fori_loop(0, half // UNROLL, some, 0)
+
+            def extra(q, carry):
+                def add(value):
+                    out[i, :, pl.ds(pl.multiple_of(q * SIDE, SIDE), SIDE)] += value
+
+                more_groups(slot, ends, i, base + q, left, bufs[i], straight, add)
+                return carry
+
+            lax.fori_loop(0, half, extra, 0)
+
+
+def pre_partials(core, x, g, table, lists, width):
+    m, depth = x.shape
+    half = width // 2
+    whole = pl.BlockSpec(memory_space=pltpu.VMEM)
+    return pl.pallas_call(
+        pre_kernel,
+        grid_spec=pltpu.PrefetchScalarGridSpec(
+            num_scalar_prefetch=3,
+            grid=(1,),
+            in_specs=[whole] * 2 + [pl.BlockSpec(memory_space=pl.ANY)] * 3,
+            out_specs=[whole] * 2,
+            scratch_shapes=[pltpu.VMEM(lists[0].shape, BF16)] * 3
+            + [pltpu.VMEM((depth // SIDE + 1, m, SIDE), BF16)] * 2
+            + [pltpu.SemaphoreType.DMA((3,))],
+        ),
+        out_shape=[jax.ShapeDtypeStruct((3, m, half), F32)] * 2,
+        compiler_params=pltpu.CompilerParams(vmem_limit_bytes=VMEM),
+        cost_estimate=pl.CostEstimate(flops=2 * m * depth * width, bytes_accessed=8_000_000, transcendentals=0),
+        name="pre_partials",
+    )(core, *table, x, g, *lists)
+
+
+def post_kernel(core_ref, slot, ends, mine_ref, other_ref, *refs):
+    lists, (keep_ref, send_ref), bufs, (hs, acc_ref, sems) = refs[:3], refs[3:5], refs[5:8], refs[8:]
+    fetch_pieces(ends, lists, bufs, sems, lambda i, copy: copy.start())
+    m = mine_ref.shape[1]
+    half = mine_ref.shape[2] // SIDE
+    core = core_ref[0]
+    for i, act in enumerate((1, 2, 0)):
+        for ref, base in ((mine_ref, half * core), (other_ref, half * (1 - core))):
+            for k in range(half):
+                hs[i, base + k] = ref[act, :, k * SIDE:(k + 1) * SIDE]
+        hs[i, 2 * half] = jnp.zeros((m, SIDE), BF16)
+    columns = ends.shape[1] - 1
+    for i, part in ((2, 0), (0, 1), (1, 1)):
+        wait_pieces(ends, lists, bufs, sems, i)
+        left, straight = hs.at[i], i == 2
+
+        def some(t, carry):
+            for u in range(UNROLL):
+                j = t * UNROLL + u
+                where = pl.ds(pl.multiple_of(j * SIDE, SIDE), SIDE)
+                value = group_dot(slot, ends, i, j, 0, left, bufs[i], straight)
+                if i == 1:
+                    value = value + acc_ref[part, :, where]
+                acc_ref[part, :, where] = value
+            return carry
+
+        lax.fori_loop(0, columns // UNROLL, some, 0)
+
+        def extra(j, carry):
+            def add(value):
+                acc_ref[part, :, pl.ds(pl.multiple_of(j * SIDE, SIDE), SIDE)] += value
+
+            more_groups(slot, ends, i, j, left, bufs[i], straight, add)
+            return carry
+
+        lax.fori_loop(0, columns, extra, 0)
+    keep_ref[...] = acc_ref[:, :m // 2]
+    send_ref[...] = acc_ref[:, m // 2:].astype(BF16)
+
+
+def post_partials(core, mine, other, table, lists, depth):
+    m, half = mine.shape[1:]
+    whole = pl.BlockSpec(memory_space=pltpu.VMEM)
+    return pl.pallas_call(
+        post_kernel,
+        grid_spec=pltpu.PrefetchScalarGridSpec(
+            num_scalar_prefetch=3,
+            grid=(1,),
+            in_specs=[whole] * 2 + [pl.BlockSpec(memory_space=pl.ANY)] * 3,
+            out_specs=[whole] * 2,
+            scratch_shapes=[pltpu.VMEM(lists[0].shape, BF16)] * 3
+            + [pltpu.VMEM((3, 2 * half // SIDE + 1, m, SIDE), BF16), pltpu.VMEM((2, m, depth), F32)]
+            + [pltpu.SemaphoreType.DMA((3,))],
+        ),
+        out_shape=[jax.ShapeDtypeStruct((2, m // 2, depth), F32), jax.ShapeDtypeStruct((2, m // 2, depth), BF16)],
+        compiler_params=pltpu.CompilerParams(vmem_limit_bytes=VMEM),
+        cost_estimate=pl.CostEstimate(flops=4 * m * depth * half, bytes_accessed=8_000_000, transcendentals=0),
+        name="post_partials",
+    )(core, *table, mine, other, *lists)
+
+
+def wgrad_kernel(core_ref, *refs, chunks, steps):
+    xs, gs, mines, others = (refs[i * chunks:(i + 1) * chunks] for i in range(4))
+    mg_ref, mu_ref, md_ref, gate_ref, up_ref, down_ref, xt_ref, g_ref = refs[4 * chunks:]
+    step = pl.program_id(0)
+    m, depth = xs[0].shape
+
+    @pl.when(step == 0)
+    def _():
+        for i in range(chunks):
+            xt_ref[:, i * m:(i + 1) * m] = xs[i][...].T
+            g_ref[i * m:(i + 1) * m, :] = gs[i][...]
+
+    acts = jnp.concatenate([jnp.where(step < steps, a[...], b[...]) for a, b in zip(mines, others)], axis=1)
+    for start in range(0, depth, TILE):
+        xt = xt_ref[start:start + TILE, :]
+        for act, scale, out in ((acts[1], mg_ref, gate_ref), (acts[2], mu_ref, up_ref)):
+            value = jnp.dot(xt, act, preferred_element_type=F32)
+            for off in range(0, TILE, SIDE):
+                block = (start + off) // SIDE
+                out[start + off:start + off + SIDE, :] = (value[off:off + SIDE] * scale[block:block + 1, :].astype(F32)).astype(BF16)
+    value = jnp.dot(acts[0].T, g_ref[...], preferred_element_type=F32)
+    for block in range(TILE // SIDE):
+        rows = slice(block * SIDE, (block + 1) * SIDE)
+        down_ref[rows, :] = (value[rows] * md_ref[0, block:block + 1, :].astype(F32)).astype(BF16)
+
+
+def weight_grads(core, xs, gs, mines, others, masks, width):
+    chunks = len(xs)
+    m, depth = xs[0].shape
+    steps = width // 2 // TILE
+    column = lambda s, c: (s + steps * c[0]) % (2 * steps)
+    spec = pltpu.PrefetchScalarGridSpec(
+        num_scalar_prefetch=1,
+        grid=(2 * steps,),
+        in_specs=[pl.BlockSpec((m, depth), lambda s, c: (0, 0))] * (2 * chunks)
+        + [pl.BlockSpec((3, m, TILE), lambda s, c: (0, 0, jnp.minimum(s, steps - 1)))] * chunks
+        + [pl.BlockSpec((3, m, TILE), lambda s, c: (0, 0, jnp.maximum(s - steps, 0)))] * chunks
+        + [
+            pl.BlockSpec((depth // SIDE, TILE), lambda s, c: (0, column(s, c))),
+            pl.BlockSpec((depth // SIDE, TILE), lambda s, c: (0, column(s, c))),
+            pl.BlockSpec((1, TILE // SIDE, depth), lambda s, c: (column(s, c), 0, 0)),
+        ],
+        out_specs=[
+            pl.BlockSpec((depth, TILE), lambda s, c: (0, column(s, c))),
+            pl.BlockSpec((depth, TILE), lambda s, c: (0, column(s, c))),
+            pl.BlockSpec((TILE, depth), lambda s, c: (column(s, c), 0)),
+        ],
+        scratch_shapes=[pltpu.VMEM((depth, chunks * m), BF16), pltpu.VMEM((chunks * m, depth), BF16)],
+    )
+    return pl.pallas_call(
+        functools.partial(wgrad_kernel, chunks=chunks, steps=steps),
+        grid_spec=spec,
+        out_shape=[
+            jax.ShapeDtypeStruct((depth, width), BF16),
+            jax.ShapeDtypeStruct((depth, width), BF16),
+            jax.ShapeDtypeStruct((width, depth), BF16),
+        ],
+        compiler_params=pltpu.CompilerParams(vmem_limit_bytes=VMEM),
+        cost_estimate=pl.CostEstimate(
+            flops=6 * chunks * m * depth * width, bytes_accessed=6 * depth * width, transcendentals=0
+        ),
+        name="weight_grads",
+    )(core, *xs, *gs, *mines, *others, *masks)
+
+
+def staged_body(tokens, grad_out, gate_weight, up_weight, down_weight, block_mask, *, wide):
+    lines = wide // 2
+    depth, width = gate_weight.shape
+    core = (lax.axis_index("narrow") % 2).astype(jnp.int32).reshape(1)
+    swap_core = [(i, i ^ 1) for i in range(4)]
+    swap_y = [(i, i ^ 2) for i in range(4)]
+    swap_x = [(i, i ^ 1) for i in range(wide)]
+    fetch = lambda d: [((i + 2 * d) % wide, i) for i in range(wide)]
+    give = lambda d: [(i, (i + 2 * d) % wide) for i in range(wide)]
+
+    stretch = lambda blocks: jnp.repeat(blocks, SIDE, axis=1).astype(BF16)
+    masks = (
+        stretch(block_mask[0]),
+        stretch(block_mask[1]),
+        stretch(block_mask[2].T).reshape(width // TILE, TILE // SIDE, depth),
+    )
+    weights = (gate_weight, up_weight, down_weight)
+
+    first = tables(jnp.stack([block_mask[0], block_mask[1], block_mask[2]]))
+    second = tables(jnp.transpose(jnp.stack([block_mask[0], block_mask[1], block_mask[2]]), (0, 2, 1)))
+    lists = pack_blocks(weights, first, second)
+
+    rows = tokens.shape[0] // CHUNKS
+    xs, gs = [], []
+    gate = None
+    for c in range(CHUNKS):
+        own = jnp.stack([tokens[c * rows:(c + 1) * rows], grad_out[c * rows:(c + 1) * rows]])
+        if gate is not None:
+            own, gate = lax.optimization_barrier((own, gate))
+        far = [lax.ppermute(own, "wide", fetch(d)) for d in range(1, lines)]
+        gate = far
+        if c == 0:
+            line = [own] + far
+            near = lax.ppermute(own, "wide", swap_x)
+            rest = lax.ppermute(jnp.stack(far), "wide", swap_x)
+            line = line + [near] + [rest[d] for d in range(lines - 1)]
+        else:
+            line = [own] + far
+            rest = lax.ppermute(jnp.stack(line), "wide", swap_x)
+            line = line + [rest[d] for d in range(lines)]
+        xs.append(jnp.concatenate([block[0] for block in line], axis=0))
+        gs.append(jnp.concatenate([block[1] for block in line], axis=0))
+
+    sums, arrived = [], []
+    for c in range(CHUNKS):
+        send, keep = pre_partials(core, xs[c], gs[c], first, lists[:3], width)
+        total = keep + lax.ppermute(send, "narrow", swap_core)
+        sums.append(total)
+        arrived.append(lax.ppermute(total.astype(BF16), "narrow", swap_y))
+
+    mines, others, finals = [], [], []
+    for c in range(CHUNKS):
+        gate_pre, up_pre, hidden_grad = sums[c] + arrived[c].astype(F32)
+        sig = jax.nn.sigmoid(gate_pre)
+        hidden = gate_pre * sig * up_pre
+        gate_grad = hidden_grad * up_pre * sig * (1.0 + gate_pre * (1.0 - sig))
+        up_grad = hidden_grad * gate_pre * sig
+        mine = jnp.stack([hidden, gate_grad, up_grad]).astype(BF16)
+        other = lax.ppermute(mine, "narrow", swap_core)
+        mines.append(mine)
+        others.append(other)
+        keep, send = post_partials(core, mine, other, second, lists[3:], depth)
+        total = keep + lax.ppermute(send, "wide", swap_x).astype(F32)
+        total = total.reshape(2, lines, rows, depth)
+        final = total[:, 0]
+        for d in range(1, lines):
+            final = final + lax.ppermute(total[:, d].astype(BF16), "wide", give(d)).astype(F32)
+        finals.append(final.astype(BF16))
+
+    gate_wgrad, up_wgrad, down_wgrad = weight_grads(core, xs, gs, mines, others, masks, width)
+    both = jnp.concatenate(finals, axis=1)
+    return (both[0], both[1], gate_wgrad, up_wgrad, down_wgrad)
+
+
 def solution(mesh):
+    wide, narrow = mesh.shape["wide"], mesh.shape["narrow"]
+
+    def body(*args):
+        tokens, gate_weight = args[0], args[2]
+        fits = narrow == 4 and wide == 8 and tokens.shape[0] % (16 * CHUNKS) == 0
+        fits = fits and gate_weight.shape[1] % (2 * TILE) == 0 and gate_weight.shape[0] % TILE == 0
+        return staged_body(*args, wide=wide) if fits else plain_body(*args)
+
     return jax.shard_map(
         body,
         mesh=mesh,

time: 677 us -> 889 us (1.31); the launches traced: 675 us -> 877 us
  Pallas kernels: 0 us -> 676 us
  waiting for transfers between devices: 444 us -> 119 us
  matrix products: 107 us -> 0 us
  local copies, waits for them, and re-layouts: 81.4 us -> 12.8 us
  starting transfers between devices: 0.2 us -> 48.7 us
  between operations: 13.9 us -> 1.97 us
  other arithmetic: 29 us -> 18.9 us
    pallas_call x0 -> x10, Pallas kernels: none -> 676 us  [the longest x1 525 us: pack_blocks(): pl.pallas_call(pack_kernel, grid_spec=pltpu.PrefetchScalarGridSpec(num_sc...]
    psum x1 -> x0, waiting for transfers between devices: 321 us -> none  [body(): gate_pre, up_pre = lax.psum((gate_part, up_part), 'narrow')]
    ppermute x0 -> x45, waiting for transfers between devices: none -> 119 us  [the longest x4 89.9 us: staged_body(): arrived.append(lax.ppermute(total.astype(BF16), 'narrow', swap_y))]
    dot_general x9 -> x0, matrix products: 107 us -> none  [the longest x3 37.5 us: contract_first(): lax.dot_general(left, right, (((0,), (0,)), ((), ())), preferred_element_...]
    reduce_scatter x2 -> x0, waiting for transfers between devices: 91.9 us -> none  [the longest x1 89.5 us: body(): lax.psum_scatter(jnp.dot(hidden, down_masked, preferred_element_type=jnp....]
    unnamed x24 -> x76, local copies, waits for them, and re-layouts: 73.1 us -> 9.11 us
    ppermute x0 -> x45, starting transfers between devices: none -> 48.7 us  [the longest x12 22.2 us: staged_body(): lax.ppermute(total[:, d].astype(BF16), 'wide', give(d)).astype(F32)]
    all_gather x2 -> x0, waiting for transfers between devices: 29.5 us -> none  [the longest x1 28.7 us: body(): lax.all_gather(grad_out, 'wide', axis=0, tiled=True)]
  transfers between devices with their start and end apart: 5 -> 45, of which waited for: 5 -> 12; matrix products, arithmetic and copies ran while one was open for 24% -> 3% of each run, Pallas kernels for 0% -> 77%
where the time goes in v1:
time: 889 us; the launch traced here: 877 us
  Pallas kernels  676 us (76%)
  waiting for transfers between devices  119 us (13%)
  starting transfers between devices  48.7 us (5%)
  other arithmetic  18.9 us (2%)
  local copies, waits for them, and re-layouts  12.8 us (1%)
    pallas_call x1, Pallas kernels, pack_blocks(): pl.pallas_call(pack_kernel, grid_spec=pltpu.PrefetchScalarGridSpec(num_sc...  525 us
    ppermute x4, waiting for transfers between devices, staged_body(): arrived.append(lax.ppermute(total.astype(BF16), 'narrow', swap_y))  89.9 us
    pallas_call x4, Pallas kernels, pre_partials(): pl.pallas_call(pre_kernel, grid_spec=pltpu.PrefetchScalarGridSpec(num_sca...  65.3 us
    pallas_call x4, Pallas kernels, post_partials(): pl.pallas_call(post_kernel, grid_spec=pltpu.PrefetchScalarGridSpec(num_sc...  58.7 us
    pallas_call x1, Pallas kernels, weight_grads(): pl.pallas_call(functools.partial(wgrad_kernel, chunks=chunks, steps=steps...  27.1 us
    ppermute x12, starting transfers between devices, staged_body(): lax.ppermute(total[:, d].astype(BF16), 'wide', give(d)).astype(F32)  22.2 us
  transfers between devices with their start and end apart: 45, of which 12 were waited for; matrix products, arithmetic and copies ran while one was open for 3% of the time, Pallas kernels for 77%

profile of v1, /device:TPU:0, one launch (start us, length us, event | category | flops | bytes accessed | tf_op | source)
XLA Modules:
  0.0 877.1 jit_solution(12514836096819412462)
XLA Ops:
  1.8 5.1 collective-permute-start
  14.3 525.0 %pack_blocks.1 = (bf16[392,128,128]{2,1,0:T(8,128)(2,1)}, bf16[392,128,128]{2,1,0:T(8,128)(2,1)}, bf16[392,128,128]{2,1,0:T(8,128)(2,1)}, bf16[392,128,128]{2,1,...) custom-call(s32[72,16]{1,0:T(8,128)} %bitcast.370, ...), custom_call_target="tpu_custom_call" | custom-call | bytes 60000000 | tf_op jit(solution)/shard_map/pack_blocks/pallas_call | solution.py:128
  541.8 4.0 collective-permute-done.12
  545.8 2.4 collective-permute-done.14
  553.2 5.2 collective-permute-done.24
  563.5 16.2 %pre_partials.4 = (f32[3,128,1536]{2,1,0:T(8,128)}, f32[3,128,1536]{2,1,0:T(8,128)}) custom-call(s32[1]{0:T(128)} %bitcast.core_ref, s32[72,16]{1,0:T(8,128)} %bitcast.371, s32[3,25]{1,0:T(4,128)} %select_reduce_fusion.2.ends1.ends, bf16[128,2048]{1,0:T(8,128)(2,1)} %copy-done.16, bf16[128,2048]{1,0:T(8,128)(2,1)} %copy-done.17, ...), custom_call_target="tpu_custom_call" | custom-call | flops 1610612736 | bytes 8000000 | tf_op jit(solution)/shard_map/pre_partials/pallas_call | solution.py:227
  582.9 16.2 %pre_partials.5 = (f32[3,128,1536]{2,1,0:T(8,128)}, f32[3,128,1536]{2,1,0:T(8,128)}) custom-call(s32[1]{0:T(128)} %bitcast.core_ref, s32[72,16]{1,0:T(8,128)} %bitcast.372, s32[3,25]{1,0:T(4,128)} %select_reduce_fusion.2.ends1.ends, bf16[128,2048]{1,0:T(8,128)(2,1)} %copy-done.19, bf16[128,2048]{1,0:T(8,128)(2,1)} %copy-done.18, ...), custom_call_target="tpu_custom_call" | custom-call | flops 1610612736 | bytes 8000000 | tf_op jit(solution)/shard_map/pre_partials/pallas_call | solution.py:227
  600.2 16.5 %pre_partials.6 = (f32[3,128,1536]{2,1,0:T(8,128)}, f32[3,128,1536]{2,1,0:T(8,128)}) custom-call(s32[1]{0:T(128)} %bitcast.core_ref, s32[72,16]{1,0:T(8,128)} %bitcast.373, s32[3,25]{1,0:T(4,128)} %select_reduce_fusion.2.ends1.ends, bf16[128,2048]{1,0:T(8,128)(2,1)} %copy-done.23, bf16[128,2048]{1,0:T(8,128)(2,1)} %copy-done.22, ...), custom_call_target="tpu_custom_call" | custom-call | flops 1610612736 | bytes 8000000 | tf_op jit(solution)/shard_map/pre_partials/pallas_call | solution.py:227
  618.0 16.3 %pre_partials.7 = (f32[3,128,1536]{2,1,0:T(8,128)}, f32[3,128,1536]{2,1,0:T(8,128)}) custom-call(s32[1]{0:T(128)} %bitcast.core_ref, s32[72,16]{1,0:T(8,128)} %bitcast.374, s32[3,25]{1,0:T(4,128)} %select_reduce_fusion.2.ends1.ends, bf16[128,2048]{1,0:T(8,128)(2,1)} %copy-done.21, bf16[128,2048]{1,0:T(8,128)(2,1)} %copy-done.20, ...), custom_call_target="tpu_custom_call" | custom-call | flops 1610612736 | bytes 8000000 | tf_op jit(solution)/shard_map/pre_partials/pallas_call | solution.py:227
  649.8 17.7 %collective-permute-done.6 = bf16[3,128,1536]{2,1,0:T(8,128)(2,1)S(1)} collective-permute-done((bf16[3,128,1536]{2,1,0:T(8,128)(2,1)S(1)}, bf16[3,128,1536]{2,1,0:T(8,128)(2,1)S(1)}, u32[]{:S(2)}, u32[]{:S(2)}) %collective-permute-start.6) | collective-permute-done | bytes 1179680 | tf_op jit(solution)/shard_map/ppermute | solution.py:419
  668.5 24.2 %collective-permute-done.17 = bf16[3,128,1536]{2,1,0:T(8,128)(2,1)S(1)} collective-permute-done((bf16[3,128,1536]{2,1,0:T(8,128)(2,1)S(1)}, bf16[3,128,1536]{2,1,0:T(8,128)(2,1)S(1)}, u32[]{:S(2)}, u32[]{:S(2)}) %collective-permute-start.17) | collective-permute-done | bytes 1179680 | tf_op jit(solution)/shard_map/ppermute | solution.py:419
  693.8 24.2 %collective-permute-done.28 = bf16[3,128,1536]{2,1,0:T(8,128)(2,1)S(1)} collective-permute-done((bf16[3,128,1536]{2,1,0:T(8,128)(2,1)S(1)}, bf16[3,128,1536]{2,1,0:T(8,128)(2,1)S(1)}, u32[]{:S(2)}, u32[]{:S(2)}) %collective-permute-start.28) | collective-permute-done | bytes 1179680 | tf_op jit(solution)/shard_map/ppermute | solution.py:419
  719.1 23.8 %collective-permute-done.39 = bf16[3,128,1536]{2,1,0:T(8,128)(2,1)S(1)} collective-permute-done((bf16[3,128,1536]{2,1,0:T(8,128)(2,1)S(1)}, bf16[3,128,1536]{2,1,0:T(8,128)(2,1)S(1)}, u32[]{:S(2)}, u32[]{:S(2)}) %collective-permute-start.39) | collective-permute-done | bytes 1179680 | tf_op jit(solution)/shard_map/ppermute | solution.py:419
  744.8 14.6 %post_partials.4 = (f32[2,64,2048]{2,1,0:T(8,128)}, bf16[2,64,2048]{2,1,0:T(8,128)(2,1)}) custom-call(s32[1]{0:T(128)} %bitcast.core_ref, s32[48,24]{1,0:T(8,128)} %bitcast.379, s32[3,17]{1,0:T(4,128)} %select_reduce_fusion.3.ends2.ends, bf16[3,128,1536]{2,1,0:T(8,128)(2,1)} %copy-done, bf16[3,128,1536]{2,1,0:T(8,128)(2,1)} %copy-done.8, ...), custom_call_target="tpu_custom_call" | custom-call | flops 1610612736 | bytes 8000000 | tf_op jit(solution)/shard_map/post_partials/pallas_call | solution.py:288
  760.8 14.8 %post_partials.5 = (f32[2,64,2048]{2,1,0:T(8,128)}, bf16[2,64,2048]{2,1,0:T(8,128)(2,1)}) custom-call(s32[1]{0:T(128)} %bitcast.core_ref, s32[48,24]{1,0:T(8,128)} %bitcast.380, s32[3,17]{1,0:T(4,128)} %select_reduce_fusion.3.ends2.ends, bf16[3,128,1536]{2,1,0:T(8,128)(2,1)} %copy-done.1, bf16[3,128,1536]{2,1,0:T(8,128)(2,1)} %copy-done.9, ...), custom_call_target="tpu_custom_call" | custom-call | flops 1610612736 | bytes 8000000 | tf_op jit(solution)/shard_map/post_partials/pallas_call | solution.py:288
  778.0 14.6 %post_partials.6 = (f32[2,64,2048]{2,1,0:T(8,128)}, bf16[2,64,2048]{2,1,0:T(8,128)(2,1)}) custom-call(s32[1]{0:T(128)} %bitcast.core_ref, s32[48,24]{1,0:T(8,128)} %bitcast.381, s32[3,17]{1,0:T(4,128)} %select_reduce_fusion.3.ends2.ends, bf16[3,128,1536]{2,1,0:T(8,128)(2,1)} %copy-done.2, bf16[3,128,1536]{2,1,0:T(8,128)(2,1)} %copy-done.10, ...), custom_call_target="tpu_custom_call" | custom-call | flops 1610612736 | bytes 8000000 | tf_op jit(solution)/shard_map/post_partials/pallas_call | solution.py:288
  797.8 27.1 %weight_grads.1 = (bf16[2048,3072]{1,0:T(8,128)(2,1)}, bf16[2048,3072]{1,0:T(8,128)(2,1)}, bf16[3072,2048]{1,0:T(8,128)(2,1)}) custom-call(s32[1]{0:T(128)} %bitcast.core_ref, bf16[128,2048]{1,0:T(8,128)(2,1)} %copy-done.16, bf16[128,2048]{1,0:T(8,128)(2,1)} %copy-done.19, bf16[128,2048]{1,0:T(8,128)(2,1)} %copy-done.23, bf16[128,2048]{1,0:T(8,128)(2,1)} %copy-done.21, ...), custom_call_target="tpu_custom_call" | custom-call | flops 19327352832 | bytes 37748736 | tf_op jit(solution)/shard_map/weight_grads/pallas_call | solution.py:355
  824.9 14.8 %post_partials.7 = (f32[2,64,2048]{2,1,0:T(8,128)}, bf16[2,64,2048]{2,1,0:T(8,128)(2,1)}) custom-call(s32[1]{0:T(128)} %bitcast.core_ref, s32[48,24]{1,0:T(8,128)} %bitcast.382, s32[3,17]{1,0:T(4,128)} %select_reduce_fusion.3.ends2.ends, bf16[3,128,1536]{2,1,0:T(8,128)(2,1)} %copy-done.3, bf16[3,128,1536]{2,1,0:T(8,128)(2,1)} %copy-done.11, ...), custom_call_target="tpu_custom_call" | custom-call | flops 1610612736 | bytes 8000000 | tf_op jit(solution)/shard_map/post_partials/pallas_call | solution.py:288
  846.2 3.1 collective-permute-done.20
  849.3 5.2 collective-permute-start.32
  854.5 3.2 collective-permute-done.21
  860.0 4.2 collective-permute-start.42
  866.6 3.7 collective-permute-done.32
  870.4 5.5 collective-permute-done.43
  (220 shorter events, 67.5 us)
Async XLA Ops:
  1.8 537.5 %collective-permute-start = (bf16[2,16,2048]{2,1,0:T(8,128)(2,1)S(1)}, bf16[2,16,2048]{2,1,0:T(8,128)(2,1)S(1)}, u32[]{:S(2)}, u32[]{:S(2)}) collective-permute-start(bf16[2,16,2048]{2,1,0:T(8,128)(2,1)S(1)} %pad_maximum_fusion.9), channel_id=1, source_target_pairs={{8,0},{12,4},{16,8},{20,12},{24,16},{28,20},{0,24},{4,28},{9,1},{1... | collective-permute-start | bytes 393224 | tf_op jit(solution)/shard_map/ppermute | solution.py:400
  6.9 532.5 %collective-permute-start.1 = (bf16[2,16,2048]{2,1,0:T(8,128)(2,1)S(1)}, bf16[2,16,2048]{2,1,0:T(8,128)(2,1)S(1)}, u32[]{:S(2)}, u32[]{:S(2)}) collective-permute-start(bf16[2,16,2048]{2,1,0:T(8,128)(2,1)S(1)} %pad_maximum_fusion.9), channel_id=1, source_target_pairs={{16,0},{20,4},{24,8},{28,12},{0,16},{4,20},{8,24},{12,28},{17,1},{... | collective-permute-start | bytes 393224 | tf_op jit(solution)/shard_map/ppermute | solution.py:400
  6.9 532.5 %collective-permute-start.2 = (bf16[2,16,2048]{2,1,0:T(8,128)(2,1)S(1)}, bf16[2,16,2048]{2,1,0:T(8,128)(2,1)S(1)}, u32[]{:S(2)}, u32[]{:S(2)}) collective-permute-start(bf16[2,16,2048]{2,1,0:T(8,128)(2,1)S(1)} %pad_maximum_fusion.9), channel_id=1, source_target_pairs={{24,0},{28,4},{0,8},{4,12},{8,16},{12,20},{16,24},{20,28},{25,1},{... | collective-permute-start | bytes 393224 | tf_op jit(solution)/shard_map/ppermute | solution.py:400
  7.9 533.9 %collective-permute-start.3 = (bf16[2,16,2048]{2,1,0:T(8,128)(2,1)S(1)}, bf16[2,16,2048]{2,1,0:T(8,128)(2,1)S(1)}, u32[]{:S(2)}, u32[]{:S(2)}) collective-permute-start(bf16[2,16,2048]{2,1,0:T(8,128)(2,1)S(1)} %pad_maximum_fusion.9), channel_id=1, source_target_pairs={{0,4},{4,0},{8,12},{12,8},{16,20},{20,16},{24,28},{28,24},{1,5},{5... | collective-permute-start | bytes 393224 | tf_op jit(solution)/shard_map/ppermute | solution.py:404
  551.7 30.1 %collective-permute-start.15 = (bf16[4,2,16,2048]{3,2,1,0:T(8,128)(2,1)S(1)}, bf16[4,2,16,2048]{3,2,1,0:T(8,128)(2,1)S(1)}, u32[]{:S(2)}, u32[]{:S(2)}) collective-permute-start(bf16[4,2,16,2048]{3,2,1,0:T(8,128)(2,1)S(1)} %pad_maximum_fusion.4), channel_id=1, source_target_pairs={{0,4},{4,0},{8,12},{12,8},{16,20},{20,16},{24,28},{28,24},{1,5},{5... | collective-permute-start | bytes 1572872 | tf_op jit(solution)/shard_map/ppermute | solution.py:409
  562.4 36.8 %collective-permute-start.26 = (bf16[4,2,16,2048]{3,2,1,0:T(8,128)(2,1)S(1)}, bf16[4,2,16,2048]{3,2,1,0:T(8,128)(2,1)S(1)}, u32[]{:S(2)}, u32[]{:S(2)}) collective-permute-start(bf16[4,2,16,2048]{3,2,1,0:T(8,128)(2,1)S(1)} %pad_maximum_fusion.5), channel_id=1, source_target_pairs={{0,4},{4,0},{8,12},{12,8},{16,20},{20,16},{24,28},{28,24},{1,5},{5... | collective-permute-start | bytes 1572872 | tf_op jit(solution)/shard_map/ppermute | solution.py:409
  579.8 56.5 %collective-permute-start.5 = (f32[3,128,1536]{2,1,0:T(8,128)}, f32[3,128,1536]{2,1,0:T(8,128)}, u32[]{:S(2)}, u32[]{:S(2)}) collective-permute-start(f32[3,128,1536]{2,1,0:T(8,128)} %get-tuple-element.37), channel_id=1, source_target_pairs={{0,1},{1,0},{2,3},{3,2},{4,5},{5,4},{6,7},{7,6},{8,9},{9,8},{10,11... | collective-permute-start | bytes 7077896 | tf_op jit(solution)/shard_map/ppermute | solution.py:417
  579.9 37.0 %collective-permute-start.37 = (bf16[4,2,16,2048]{3,2,1,0:T(8,128)(2,1)S(1)}, bf16[4,2,16,2048]{3,2,1,0:T(8,128)(2,1)S(1)}, u32[]{:S(2)}, u32[]{:S(2)}) collective-permute-start(bf16[4,2,16,2048]{3,2,1,0:T(8,128)(2,1)S(1)} %pad_maximum_fusion.6), channel_id=1, source_target_pairs={{0,4},{4,0},{8,12},{12,8},{16,20},{20,16},{24,28},{28,24},{1,5},{5... | collective-permute-start | bytes 1572872 | tf_op jit(solution)/shard_map/ppermute | solution.py:409
  599.1 39.6 %collective-permute-start.16 = (f32[3,128,1536]{2,1,0:T(8,128)}, f32[3,128,1536]{2,1,0:T(8,128)}, u32[]{:S(2)}, u32[]{:S(2)}) collective-permute-start(f32[3,128,1536]{2,1,0:T(8,128)} %get-tuple-element.45), channel_id=1, source_target_pairs={{0,1},{1,0},{2,3},{3,2},{4,5},{5,4},{6,7},{7,6},{8,9},{9,8},{10,11... | collective-permute-start | bytes 7077896 | tf_op jit(solution)/shard_map/ppermute | solution.py:417
  616.8 26.4 %collective-permute-start.27 = (f32[3,128,1536]{2,1,0:T(8,128)}, f32[3,128,1536]{2,1,0:T(8,128)}, u32[]{:S(2)}, u32[]{:S(2)}) collective-permute-start(f32[3,128,1536]{2,1,0:T(8,128)} %get-tuple-element.50), channel_id=1, source_target_pairs={{0,1},{1,0},{2,3},{3,2},{4,5},{5,4},{6,7},{7,6},{8,9},{9,8},{10,11... | collective-permute-start | bytes 7077896 | tf_op jit(solution)/shard_map/ppermute | solution.py:417
  638.6 28.8 %collective-permute-start.6 = (bf16[3,128,1536]{2,1,0:T(8,128)(2,1)S(1)}, bf16[3,128,1536]{2,1,0:T(8,128)(2,1)S(1)}, u32[]{:S(2)}, u32[]{:S(2)}) collective-permute-start(bf16[3,128,1536]{2,1,0:T(8,128)(2,1)S(1)} %get-tuple-element.61), channel_id=1, source_target_pairs={{0,2},{1,3},{2,0},{3,1},{4,6},{5,7},{6,4},{7,5},{8,10},{9,11},{10,... | collective-permute-start | bytes 3538952 | tf_op jit(solution)/shard_map/ppermute | solution.py:419
  641.1 51.7 %collective-permute-start.17 = (bf16[3,128,1536]{2,1,0:T(8,128)(2,1)S(1)}, bf16[3,128,1536]{2,1,0:T(8,128)(2,1)S(1)}, u32[]{:S(2)}, u32[]{:S(2)}) collective-permute-start(bf16[3,128,1536]{2,1,0:T(8,128)(2,1)S(1)} %get-tuple-element.63), channel_id=1, source_target_pairs={{0,2},{1,3},{2,0},{3,1},{4,6},{5,7},{6,4},{7,5},{8,10},{9,11},{10,... | collective-permute-start | bytes 3538952 | tf_op jit(solution)/shard_map/ppermute | solution.py:419
  645.4 72.6 %collective-permute-start.28 = (bf16[3,128,1536]{2,1,0:T(8,128)(2,1)S(1)}, bf16[3,128,1536]{2,1,0:T(8,128)(2,1)S(1)}, u32[]{:S(2)}, u32[]{:S(2)}) collective-permute-start(bf16[3,128,1536]{2,1,0:T(8,128)(2,1)S(1)} %get-tuple-element.65), channel_id=1, source_target_pairs={{0,2},{1,3},{2,0},{3,1},{4,6},{5,7},{6,4},{7,5},{8,10},{9,11},{10,... | collective-permute-start | bytes 3538952 | tf_op jit(solution)/shard_map/ppermute | solution.py:419
  647.7 95.2 %collective-permute-start.39 = (bf16[3,128,1536]{2,1,0:T(8,128)(2,1)S(1)}, bf16[3,128,1536]{2,1,0:T(8,128)(2,1)S(1)}, u32[]{:S(2)}, u32[]{:S(2)}) collective-permute-start(bf16[3,128,1536]{2,1,0:T(8,128)(2,1)S(1)} %get-tuple-element.67), channel_id=1, source_target_pairs={{0,2},{1,3},{2,0},{3,1},{4,6},{5,7},{6,4},{7,5},{8,10},{9,11},{10,... | collective-permute-start | bytes 3538952 | tf_op jit(solution)/shard_map/ppermute | solution.py:419
  668.5 75.3 %collective-permute-start.7 = (bf16[3,128,1536]{2,1,0:T(8,128)(2,1)S(1)}, bf16[3,128,1536]{2,1,0:T(8,128)(2,1)S(1)}, u32[]{:S(2)}, u32[]{:S(2)}) collective-permute-start(bf16[3,128,1536]{2,1,0:T(8,128)(2,1)S(1)} %pad_maximum_fusion.mine_ref.refs_8_), channel_id=1, source_target_pairs={{0,1},{1,0},{2,3},{3,2},{4,5},{5,4},{6,7},{7,6},{8,9},{9,8},{10,11... | collective-permute-start | bytes 3538952 | tf_op jit(solution)/shard_map/ppermute | solution.py:429
  693.7 65.9 %collective-permute-start.18 = (bf16[3,128,1536]{2,1,0:T(8,128)(2,1)S(1)}, bf16[3,128,1536]{2,1,0:T(8,128)(2,1)S(1)}, u32[]{:S(2)}, u32[]{:S(2)}) collective-permute-start(bf16[3,128,1536]{2,1,0:T(8,128)(2,1)S(1)} %pad_maximum_fusion.1.mine_ref.refs_9_), channel_id=1, source_target_pairs={{0,1},{1,0},{2,3},{3,2},{4,5},{5,4},{6,7},{7,6},{8,9},{9,8},{10,11... | collective-permute-start | bytes 3538952 | tf_op jit(solution)/shard_map/ppermute | solution.py:429
  719.0 57.9 %collective-permute-start.29 = (bf16[3,128,1536]{2,1,0:T(8,128)(2,1)S(1)}, bf16[3,128,1536]{2,1,0:T(8,128)(2,1)S(1)}, u32[]{:S(2)}, u32[]{:S(2)}) collective-permute-start(bf16[3,128,1536]{2,1,0:T(8,128)(2,1)S(1)} %pad_maximum_fusion.2.mine_ref.refs_10_), channel_id=1, source_target_pairs={{0,1},{1,0},{2,3},{3,2},{4,5},{5,4},{6,7},{7,6},{8,9},{9,8},{10,11... | collective-permute-start | bytes 3538952 | tf_op jit(solution)/shard_map/ppermute | solution.py:429
  759.4 33.3 %collective-permute-start.8 = (bf16[2,64,2048]{2,1,0:T(8,128)(2,1)}, bf16[2,64,2048]{2,1,0:T(8,128)(2,1)}, u32[]{:S(2)}, u32[]{:S(2)}) collective-permute-start(bf16[2,64,2048]{2,1,0:T(8,128)(2,1)} %get-tuple-element.42), channel_id=1, source_target_pairs={{0,4},{4,0},{8,12},{12,8},{16,20},{20,16},{24,28},{28,24},{1,5},{5... | collective-permute-start | bytes 1572872 | tf_op jit(solution)/shard_map/ppermute | solution.py:433
  759.6 37.1 %collective-permute-start.40 = (bf16[3,128,1536]{2,1,0:T(8,128)(2,1)S(1)}, bf16[3,128,1536]{2,1,0:T(8,128)(2,1)S(1)}, u32[]{:S(2)}, u32[]{:S(2)}) collective-permute-start(bf16[3,128,1536]{2,1,0:T(8,128)(2,1)S(1)} %pad_maximum_fusion.3.mine_ref.refs_11_), channel_id=1, source_target_pairs={{0,1},{1,0},{2,3},{3,2},{4,5},{5,4},{6,7},{7,6},{8,9},{9,8},{10,11... | collective-permute-start | bytes 3538952 | tf_op jit(solution)/shard_map/ppermute | solution.py:429
  775.6 65.2 %collective-permute-start.19 = (bf16[2,64,2048]{2,1,0:T(8,128)(2,1)}, bf16[2,64,2048]{2,1,0:T(8,128)(2,1)S(1)}, u32[]{:S(2)}, u32[]{:S(2)}) collective-permute-start(bf16[2,64,2048]{2,1,0:T(8,128)(2,1)} %get-tuple-element.47), channel_id=1, source_target_pairs={{0,4},{4,0},{8,12},{12,8},{16,20},{20,16},{24,28},{28,24},{1,5},{5... | collective-permute-start | bytes 1572872 | tf_op jit(solution)/shard_map/ppermute | solution.py:433
  792.6 53.2 %collective-permute-start.30 = (bf16[2,64,2048]{2,1,0:T(8,128)(2,1)}, bf16[2,64,2048]{2,1,0:T(8,128)(2,1)S(1)}, u32[]{:S(2)}, u32[]{:S(2)}) collective-permute-start(bf16[2,64,2048]{2,1,0:T(8,128)(2,1)} %get-tuple-element.52), channel_id=1, source_target_pairs={{0,4},{4,0},{8,12},{12,8},{16,20},{20,16},{24,28},{28,24},{1,5},{5... | collective-permute-start | bytes 1572872 | tf_op jit(solution)/shard_map/ppermute | solution.py:433
  793.9 45.8 %collective-permute-start.10 = (bf16[2,16,2048]{2,1,0:T(8,128)(2,1)S(1)}, bf16[2,16,2048]{2,1,0:T(8,128)(2,1)S(1)}, u32[]{:S(2)}, u32[]{:S(2)}) collective-permute-start(bf16[2,16,2048]{2,1,0:T(8,128)(2,1)S(1)} %get-tuple-element.87), channel_id=1, source_target_pairs={{0,16},{4,20},{8,24},{12,28},{16,0},{20,4},{24,8},{28,12},{1,17},{... | collective-permute-start | bytes 393224 | tf_op jit(solution)/shard_map/ppermute | solution.py:437
  795.1 45.6 %collective-permute-start.11 = (bf16[2,16,2048]{2,1,0:T(8,128)(2,1)S(1)}, bf16[2,16,2048]{2,1,0:T(8,128)(2,1)S(1)}, u32[]{:S(2)}, u32[]{:S(2)}) collective-permute-start(bf16[2,16,2048]{2,1,0:T(8,128)(2,1)S(1)} %get-tuple-element.86), channel_id=1, source_target_pairs={{0,24},{4,28},{8,0},{12,4},{16,8},{20,12},{24,16},{28,20},{1,25},{... | collective-permute-start | bytes 393224 | tf_op jit(solution)/shard_map/ppermute | solution.py:437
  796.7 44.1 %collective-permute-start.9 = (bf16[2,16,2048]{2,1,0:T(8,128)(2,1)S(1)}, bf16[2,16,2048]{2,1,0:T(8,128)(2,1)S(1)}, u32[]{:S(2)}, u32[]{:S(2)}) collective-permute-start(bf16[2,16,2048]{2,1,0:T(8,128)(2,1)S(1)} %get-tuple-element.85), channel_id=1, source_target_pairs={{0,8},{4,12},{8,16},{12,20},{16,24},{20,28},{24,0},{28,4},{1,9},{5... | collective-permute-start | bytes 393224 | tf_op jit(solution)/shard_map/ppermute | solution.py:437
  (45 other events, 468.1 us)
